TPU v7x, 256 devices: a whole 4x4x8 slice. The times are simulated.
256 devices in a mesh: dp: 64 (over z, y_lo, x), tensor: 4 (over y_hi, core).
Axes of the slice: x: 4, y: 4 (y_hi: 2, y_lo: 2; y = y_hi * 2 + y_lo), z: 8, core: 2. Of those that a mesh axis runs over, the one named last changes fastest.
Arguments:
- activations: bfloat16 [8192, 4096], P('dp'), may hold values from -6 to 6
- grad_out: bfloat16 [8192, 14336], P('dp', 'tensor'), may hold values from -16 to 16
- weight_codes: int32 [4096, 14336], P('dp', 'tensor'), may hold values from 0 to 15
- scales: bfloat16 [32, 14336], P(None, 'tensor'), may hold values from 0.00049972534 to 0.0079956055
- zero_points: int32 [32, 14336], P(None, 'tensor'), may hold values from 0 to 15
Outputs:
- grad_inputs: bfloat16 [8192, 4096], P('dp', 'tensor')
- grad_log_scales: float32 [32, 4, 3584], P(None, 'tensor', 'dp')
- grad_zero_points: float32 [32, 4, 3584], P(None, 'tensor', 'dp')
Inputs may be any that keep to these rules, and one draw needn't show every extreme that they name: `weight_codes`: codes of the 4-bit weight.
All inputs are finite; a program needn't handle non-finite values.
Results may differ from a plain program's by a relative error of at most 0.012.
Values may be sent and summed in bfloat16 or wider, within the bound.
A program may use at most 128 MiB of HBM per device.

v0:
```python
import math

import jax
import jax.numpy as jnp
from jax import lax
from jax.sharding import PartitionSpec as P

GROUP = 128


def group_onehot(first_row, row_count, groups):
    row_ids = first_row + lax.iota(jnp.int32, row_count)
    group_ids = lax.iota(jnp.int32, groups)
    return (row_ids[None, :] // GROUP == group_ids[:, None]).astype(jnp.float32)


def dequantize(weight_codes, scales, zero_points):
    row_count = weight_codes.shape[0]
    first_row = lax.axis_index("dp") * row_count
    picker = group_onehot(first_row, row_count, scales.shape[0]).T.astype(jnp.bfloat16)
    scale_rows = jnp.dot(picker, scales, preferred_element_type=jnp.float32)
    zero_rows = jnp.dot(
        picker, zero_points.astype(jnp.bfloat16), preferred_element_type=jnp.float32
    )
    return (scale_rows * (weight_codes.astype(jnp.float32) - zero_rows)).astype(jnp.bfloat16)


def add_groups(total, values, first_row):
    summed = values.sum(axis=0, keepdims=True)
    group_row = first_row // GROUP
    current = lax.dynamic_slice_in_dim(total, group_row, 1, 0)
    return lax.dynamic_update_slice_in_dim(total, current + summed, group_row, 0)


def make_fold(activations, grad_cols, shard_rows, carried, piece):
    row_count = piece.shape[0]
    block_rows = math.gcd(row_count, 512)
    block_rows = math.gcd(math.gcd(block_rows, shard_rows), GROUP)

    def one_block(block_no, running):
        first_row = block_no * block_rows
        weight_rows = lax.dynamic_slice_in_dim(piece, block_no * block_rows, block_rows, 0)
        act_cols = lax.dynamic_slice_in_dim(activations, first_row, block_rows, 1)
        back_term = lax.dot_general(
            grad_cols, weight_rows, (((1,), (1,)), ((), ())), preferred_element_type=jnp.float32
        )
        input_terms = running[0]
        current = lax.dynamic_slice_in_dim(input_terms, first_row, block_rows, 1)
        input_terms = lax.dynamic_update_slice_in_dim(
            input_terms, current + back_term, first_row, 1
        )
        grad_weight = lax.dot_general(
            act_cols, grad_cols, (((0,), (0,)), ((), ())), preferred_element_type=jnp.float32
        )
        log_terms = add_groups(running[1], grad_weight * weight_rows.astype(jnp.float32), first_row)
        sum_terms = add_groups(running[2], grad_weight, first_row)
        return (input_terms, log_terms, sum_terms)

    return lax.fori_loop(0, row_count // block_rows, one_block, carried)


def on_device(activations, grad_out, weight_codes, scales, zero_points):
    dp_count = lax.axis_size("dp")
    groups = scales.shape[0]
    columns = weight_codes.shape[1]
    shard_rows = weight_codes.shape[0]
    col_share = columns // dp_count
    weight = dequantize(weight_codes, scales, zero_points)
    input_terms = jnp.zeros((activations.shape[0], activations.shape[1]), jnp.float32)
    empty = jnp.zeros((groups, columns), jnp.float32)
    start_state = (input_terms, empty, empty)
    result = make_fold(
        activations,
        grad_out,
        shard_rows,
        start_state,
        lax.all_gather(weight, "dp", axis=0, tiled=True),
    )
    input_terms = result[0]
    sum_terms = result[2]
    log_share, sum_share = (
        lax.psum_scatter(result[1], "dp", scatter_dimension=1, tiled=True),
        lax.psum_scatter(sum_terms, "dp", scatter_dimension=1, tiled=True),
    )
    feature_grad = lax.psum_scatter(
        input_terms.astype(jnp.bfloat16), "tensor", scatter_dimension=1, tiled=True
    )
    scale_share = lax.dynamic_slice_in_dim(
        scales, lax.axis_index("dp") * col_share, col_share, 1
    ).astype(jnp.float32)
    zero_grad = -scale_share * sum_share
    return (feature_grad, log_share[:, None, :], zero_grad[:, None, :])


def solution(mesh):
    in_specs = (
        P("dp", None),
        P("dp", "tensor"),
        P("dp", "tensor"),
        P(None, "tensor"),
        P(None, "tensor"),
    )
    out_specs = (P("dp", "tensor"), P(None, "tensor", "dp"), P(None, "tensor", "dp"))
    return jax.shard_map(
        on_device, mesh=mesh, in_specs=in_specs, out_specs=out_specs, check_vma=False
    )
```

profile of v0, /device:TPU:1, one launch (start us, length us, event | category | flops | bytes accessed | tf_op | source)
XLA Modules:
  0.0 1389.2 jit_solution(13716820147081365392)
XLA Ops:
  8.5 2.4 fusion.8
  11.0 333.3 %all-gather.2.cloned.1.call-done = bf16[4096,3584]{1,0:T(8,128)(2,1)} async-done(((bf16[64,3584]{1,0:T(8,128)(2,1)}), bf16[4096,3584]{1,0:T(8,128)(2,1)}) %all-gather.2.cloned.1.call-update) | async-done | bytes 29360144 | tf_op jit(solution)/shard_map/all_gather | solution.py:77
  345.3 375.7 %while.19 = (s32[]{:T(128)}, f32[128,4096]{0,1:T(8,128)S(1)}, f32[32,3584]{1,0:T(8,128)S(1)}, f32[32,3584]{1,0:T(8,128)}, bf16[4096,3584]{1,0:T(8,128)(2,1)}, /*...) while((s32[]{:T(128)}, f32[128,4096]{0,1:T(8,128)S(1)}, ...), condition=%wide.region_3.4_spmd, body=%wide.region_0.3_spmd.sunk | while | flops 118366208 | bytes 3025270 | solution.py:59
  535.9 1.6 dynamic_update_slice.36
  541.8 1.6 dynamic_update_slice.36
  547.7 1.6 dynamic_update_slice.36
  553.5 1.6 dynamic_update_slice.36
  559.4 1.6 dynamic_update_slice.36
  565.3 1.6 dynamic_update_slice.36
  571.1 1.6 dynamic_update_slice.36
  577.0 1.6 dynamic_update_slice.36
  582.9 1.6 dynamic_update_slice.36
  588.8 1.6 dynamic_update_slice.36
  606.4 1.6 dynamic_update_slice.36
  629.8 1.6 dynamic_update_slice.36
  635.7 1.6 dynamic_update_slice.36
  641.6 1.6 dynamic_update_slice.36
  647.5 1.6 dynamic_update_slice.36
  653.4 1.6 dynamic_update_slice.36
  659.2 1.6 dynamic_update_slice.36
  665.1 1.6 dynamic_update_slice.36
  671.0 1.6 dynamic_update_slice.36
  676.9 1.6 dynamic_update_slice.36
  682.7 1.6 dynamic_update_slice.36
  688.6 1.6 dynamic_update_slice.36
  694.5 1.6 dynamic_update_slice.36
  700.4 1.6 dynamic_update_slice.36
  706.3 1.6 dynamic_update_slice.36
  712.1 1.6 dynamic_update_slice.36
  718.0 1.6 dynamic_update_slice.36
  724.6 577.3 %all-reduce.5.cloned.1.call-done = (f32[32,3584]{1,0:T(8,128)}, f32[32,3584]{1,0:T(8,128)}) async-done(((f32[32,3584]{1,0:T(8,128)}, f32[32,3584]{1,0:T(8,128)}), (f32[32,3584]{1,0:T(8,128)}, f32[32,3584]{1,0:T(8,128)})) %all-reduce.5.cloned.1.call-update) | async-done | bytes 917520
  1303.4 79.3 %reduce-scatter.4.cloned.1.call-done = bf16[128,1024]{1,0:T(8,128)(2,1)} async-done(((bf16[128,4096]{1,0:T(8,128)(2,1)}), bf16[128,1024]{1,0:T(8,128)(2,1)}) %reduce-scatter.4.cloned.1.call-update) | async-done | bytes 262160 | tf_op jit(solution)/shard_map/reduce_scatter | solution.py:85
  (313 shorter events, 335.4 us)
Async XLA Ops:
  7.2 337.2 %all-gather.2.cloned.1.call-start = ((), (), s32[]{:S(2)}) async-start(), calls=%async_computation.1 | async-start | bytes 29818880 | tf_op jit(solution)/shard_map/all_gather | solution.py:77
  10.9 334.4 %copy-start = (bf16[128,3584]{1,0:T(8,128)(2,1)S(1)}, bf16[128,3584]{1,0:T(8,128)(2,1)}, u32[]{:S(2)}) copy-start(bf16[128,3584]{1,0:T(8,128)(2,1)} %param.8) | copy-start | bytes 2752516
  11.0 1291.0 %all-reduce.5.cloned.1.call-start = ((), (), s32[]{:S(2)}) async-start(), calls=%async_computation.3 | async-start | bytes 1835008
  721.1 0.8 copy-start.1
  721.9 660.8 %reduce-scatter.4.cloned.1.call-start = ((), (), s32[]{:S(2)}) async-start(), calls=%async_computation.2 | async-start | bytes 1310720 | tf_op jit(solution)/shard_map/reduce_scatter | solution.py:85
  721.9 1.5 copy-start.2
Sparse Core Ops, SparseCore 0:
  11.1 333.2 all-gather.1
  722.0 579.8 all-reduce.4
  1305.5 77.1 reduce-scatter.3
where the time goes:
time: 1400 us; the launch traced here: 1390 us
  waiting for transfers between devices  990 us (71%)
  matrix products  191 us (14%)
  local copies, waits for them, and re-layouts  128 us (9%)
  other arithmetic  61.8 us (4%)
  between operations  14.5 us (1%)
    unnamed x4, waiting for transfers between devices  577 us
    all_gather x1, waiting for transfers between devices, on_device(): lax.all_gather(weight, 'dp', axis=0, tiled=True)  333 us
    dynamic_update_slice x128, local copies, waits for them, and re-layouts, add_groups(): lax.dynamic_update_slice_in_dim(total, current + summed, group_row, 0)  124 us
    dot_general x64, matrix products, one_block(): lax.dot_general(act_cols, grad_cols, (((0,), (0,)), ((), ())), preferred_...  94.4 us
    dot_general x64, matrix products, one_block(): lax.dot_general(grad_cols, weight_rows, (((1,), (1,)), ((), ())), preferr...  92.9 us
    reduce_scatter x1, waiting for transfers between devices, on_device(): lax.psum_scatter(input_terms.astype(jnp.bfloat16), 'tensor', scatter_dime...  79.3 us
    add x64, other arithmetic, add_groups(): current + summed  60.3 us
  transfers between devices with their start and end apart: 3, of which 3 were waited for; matrix products, arithmetic and copies ran while one was open for 0% of the time, Pallas kernels for 0%

commit v1 on v0

v1 whole, which is shorter than its diff:
```python
import jax
import jax.numpy as jnp
from jax import lax
from jax.sharding import Mesh, PartitionSpec as P

GROUP = 128
NZ, NL, NX, NH, NK = 8, 2, 4, 2, 2


def dequantize(weight_codes, scales, zero_points, dp):
    rows = weight_codes.shape[0]
    group = dp * rows // GROUP
    scale_row = lax.dynamic_slice_in_dim(scales, group, 1, 0).astype(jnp.float32)
    zero_row = lax.dynamic_slice_in_dim(zero_points, group, 1, 0)
    return (scale_row * (weight_codes - zero_row).astype(jnp.float32)).astype(jnp.bfloat16)


def on_device(activations, grad_out, weight_codes, scales, zero_points):
    iz, il, ix = lax.axis_index("z"), lax.axis_index("l"), lax.axis_index("x")
    dp = (iz * NL + il) * NX + ix
    tokens, features = activations.shape
    rows, cols = weight_codes.shape
    half = cols // NL
    groups = scales.shape[0]
    weight = dequantize(weight_codes, scales, zero_points, dp)
    w = lax.all_to_all(weight.reshape(rows, NL, half), "l", 1, 0, tiled=False)
    go = lax.all_to_all(grad_out.reshape(tokens, NL, half), "l", 1, 0, tiled=False)
    w = w.reshape(NL * rows, half)
    go = go.reshape(NL * tokens, half)
    w = lax.all_gather(w, "z", axis=0, tiled=True)
    go = lax.all_gather(go, "x", axis=0, tiled=True)
    act = activations.reshape(tokens, NZ * NL, NX, rows)
    act = lax.all_to_all(act, "x", 2, 0, tiled=False)
    act = lax.all_gather(act, "l", axis=1, tiled=False)
    act = act.reshape(NX * NL * tokens, NZ * NL * rows)

    out = lax.dot_general(go, w, (((1,), (1,)), ((), ())), preferred_element_type=jnp.float32)
    out = out.astype(jnp.bfloat16).reshape(NX, NL, tokens, NH * NK, 2 * NL * rows)
    out = jnp.transpose(out, (1, 3, 0, 2, 4))
    out = out.reshape(NL * NH * NK, NX, tokens, 2 * NL * rows)
    out = lax.psum_scatter(out, ("l", "h", "k"), scatter_dimension=0, tiled=True)[0]
    out = lax.all_to_all(out, "x", 0, 0, tiled=False)
    out = out.reshape(NX, tokens, 2 * NL, rows)
    feature_grad = jnp.transpose(out, (1, 2, 0, 3)).reshape(tokens, features // 4)

    gw = lax.dot_general(act, go, (((0,), (0,)), ((), ())), preferred_element_type=jnp.float32)
    log_part = (gw * w.astype(jnp.float32)).reshape(NZ * NL, rows, half).sum(axis=1)
    sum_part = gw.reshape(NZ * NL, rows, half).sum(axis=1)
    parts = jnp.stack([log_part, sum_part]).reshape(2, NZ, NL, half)
    parts = lax.all_to_all(parts, "z", 1, 0, tiled=False).sum(axis=0)
    width = cols // (NZ * NL * NX)
    dests = half // width
    parts = jnp.transpose(parts.reshape(2, NL, dests, width), (2, 0, 1, 3))
    full = jnp.zeros((NL * dests, 2, NL, width), jnp.float32)
    full = lax.dynamic_update_slice(full, parts, (il * dests, 0, 0, 0))
    share = lax.all_to_all(full, ("z", "l", "x"), 0, 0, tiled=True)
    share = share.reshape(NZ, NL, NX // 2, 2, 2, NL, width).sum(axis=(1, 3))
    share = jnp.transpose(share, (2, 0, 3, 1, 4)).reshape(2, groups, width)
    scale_share = lax.dynamic_slice_in_dim(scales, dp * width, width, 1).astype(jnp.float32)
    return (feature_grad, share[0][:, None, :], (-scale_share * share[1])[:, None, :])


def solution(mesh):
    fine = Mesh(mesh.devices.reshape(NZ, NL, NX, NH, NK), ("z", "l", "x", "h", "k"))
    dp, tensor = ("z", "l", "x"), ("h", "k")
    in_specs = (P(dp, None), P(dp, tensor), P(dp, tensor), P(None, tensor), P(None, tensor))
    out_specs = (P(dp, tensor), P(None, tensor, dp), P(None, tensor, dp))
    return jax.shard_map(
        on_device, mesh=fine, in_specs=in_specs, out_specs=out_specs, check_vma=False
    )
```

time: 1400 us -> 247 us (0.18)
  waiting for transfers between devices: 990 us -> 125 us
  matrix products: 191 us -> 16.3 us
  local copies, waits for them, and re-layouts: 128 us -> 21.3 us
  other arithmetic: 61.8 us -> 4.14 us
  blocking collectives: 0 us -> 46.5 us
  starting transfers between devices: 0.12 us -> 16.7 us
    unnamed x4, waiting for transfers between devices: 577 us -> 0.07 us
    all_gather x1 -> x3, waiting for transfers between devices: 333 us -> 102 us  [the longest x1 53.3 us: on_device(): w = lax.all_gather(w, 'z', axis=0, tiled=True)]
    dot_general x130 -> x2, matrix products: 191 us -> 16.3 us  [the longest x1 8.45 us: on_device(): lax.dot_general(go, w, (((1,), (1,)), ((), ())), preferred_element_type=j...]
    dynamic_update_slice x128 -> x1, local copies, waits for them, and re-layouts: 124 us -> 0.07 us  [on_device(): full = lax.dynamic_update_slice(full, parts, (il * dests, 0, 0, 0))]
    reduce_scatter x1, waiting for transfers between devices: 79.3 us -> 0.01 us  [on_device(): lax.psum_scatter(out, ('l', 'h', 'k'), scatter_dimension=0, tiled=True)[0]]
    add x64 -> x0, other arithmetic: 60.3 us -> none  [add_groups(): current + summed]
    all_to_all x0 -> x3, blocking collectives: none -> 46.5 us  [the longest x1 25.4 us: on_device(): act = lax.all_to_all(act, 'x', 2, 0, tiled=False)]
    all_to_all x0 -> x3, waiting for transfers between devices: none -> 23.3 us  [the longest x1 9.76 us: on_device(): parts = lax.all_to_all(parts, 'z', 1, 0, tiled=False).sum(axis=0)]
  transfers between devices with their start and end apart: 3 -> 7, of which waited for: 3 -> 6; matrix products, arithmetic and copies ran while one was open for 0% -> 15% of each run, Pallas kernels for 0% -> 0%
where the time goes in v1:
time: 247 us; the launch traced here: 244 us
  waiting for transfers between devices  125 us (51%)
  blocking collectives  46.5 us (19%)
  local copies, waits for them, and re-layouts  21.3 us (9%)
  starting transfers between devices  16.7 us (7%)
  matrix products  16.3 us (7%)
  between operations  14 us (6%)
  other arithmetic  4.14 us (2%)
    all_gather x1, waiting for transfers between devices, on_device(): w = lax.all_gather(w, 'z', axis=0, tiled=True)  53.3 us
    all_gather x1, waiting for transfers between devices, on_device(): go = lax.all_gather(go, 'x', axis=0, tiled=True)  25.7 us
    all_to_all x1, blocking collectives, on_device(): act = lax.all_to_all(act, 'x', 2, 0, tiled=False)  25.4 us
    all_gather x1, waiting for transfers between devices, on_device(): act = lax.all_gather(act, 'l', axis=1, tiled=False)  22.8 us
    all_to_all x1, blocking collectives, on_device(): lax.all_to_all(grad_out.reshape(tokens, NL, half), 'l', 1, 0, tiled=False)  12.9 us
    all_to_all x1, waiting for transfers between devices, on_device(): parts = lax.all_to_all(parts, 'z', 1, 0, tiled=False).sum(axis=0)  9.76 us
    all_to_all x1, waiting for transfers between devices, on_device(): share = lax.all_to_all(full, ('z', 'l', 'x'), 0, 0, tiled=True)  9.41 us
    dot_general x1, matrix products, on_device(): lax.dot_general(go, w, (((1,), (1,)), ((), ())), preferred_element_type=j...  8.45 us
  transfers between devices with their start and end apart: 7, of which 6 were waited for; matrix products, arithmetic and copies ran while one was open for 15% of the time, Pallas kernels for 0%

profile of v1, /device:TPU:1, one launch (start us, length us, event | category | flops | bytes accessed | tf_op | source)
XLA Modules:
  0.0 244.2 jit_solution(2577842921177063314)
XLA Ops:
  7.2 1.6 copy.39
  8.9 12.9 %all_to_all.64 = bf16[1,128,2,1792]{1,3,0,2:T(8,128)(2,1)S(1)} all-to-all(bf16[1,128,2,1792]{1,3,0,2:T(8,128)(2,1)S(1)} %bitcast.57), channel_id=1, replica_groups=mesh['z'=8,'l'=2,'x'=4,'h'=2,'k'=2] {'l'}, dimensions={2} | all-to-all | bytes 1835008 | tf_op jit(solution)/shard_map/all_to_all | solution.py:27
  21.8 1.3 copy.41
  23.2 0.9 convert_reduce_fusion
  24.1 0.1 multiply_convert_fusion
  24.4 8.2 %all_to_all.65 = bf16[1,64,2,1792]{3,1,0,2:T(8,128)(2,1)} all-to-all(bf16[1,64,2,1792]{3,1,0,2:T(8,128)(2,1)S(1)} %copy.38), channel_id=1, replica_groups=mesh['z'=8,'l'=2,'x'=4,'h'=2,'k'=2] {'l'}, dimensions={2} | all-to-all | bytes 917504 | tf_op jit(solution)/shard_map/all_to_all | solution.py:26
  32.7 0.7 copy.45
  33.5 25.4 %all_to_all.66 = bf16[1,128,16,4,64]{1,4,2,0,3:T(8,128)(2,1)} all-to-all(bf16[1,128,16,4,64]{1,4,2,0,3:T(8,128)(2,1)S(1)} %copy.46), channel_id=1, replica_groups=mesh['z'=8,'l'=2,'x'=4,'h'=2,'k'=2] {'x'}, dimensions={3} | all-to-all | bytes 2097152 | tf_op jit(solution)/shard_map/all_to_all | solution.py:33
  58.9 25.7 %all-gather.7.cloned.1.call-done = bf16[1024,1792]{1,0:T(8,128)(2,1)} async-done(((bf16[256,1792]{1,0:T(8,128)(2,1)}), bf16[1024,1792]{1,0:T(8,128)(2,1)}) %all-gather.7.cloned.1.call-update) | async-done | bytes 3670032 | tf_op jit(solution)/shard_map/all_gather | solution.py:31
  84.7 53.3 %all-gather.5.cloned.1.call-done = bf16[1024,1792]{1,0:T(8,128)(2,1)} async-done(((bf16[128,1792]{1,0:T(8,128)(2,1)}), bf16[1024,1792]{1,0:T(8,128)(2,1)}) %all-gather.5.cloned.1.call-update) | async-done | bytes 3670032 | tf_op jit(solution)/shard_map/all_gather | solution.py:30
  138.0 8.4 %convert_bitcast_fusion = bf16[1024,1024]{0,1:T(8,128)(2,1)} fusion(bf16[1024,1792]{1,0:T(8,128)(2,1)} %all-gather.5.cloned.1.call-done, bf16[1024,1792]{1,0:T(8,128)(2,1)} %all-gather.7.cloned.1.call-done), kind=kOutput, calls=%fused_computation.3 | convolution fusion | flops 3759144960 | bytes 9437184 | tf_op jit(solution)/shard_map/dot_general | solution.py:37
  146.4 3.2 %reshape.46 = bf16[4,2,128,4,256]{2,1,0,4,3:T(2,128)(2,1)S(1)} reshape(bf16[1024,1024]{0,1:T(8,128)(2,1)} %convert_bitcast_fusion) | data formatting | bytes 4194304 | tf_op jit(solution)/shard_map/reshape | solution.py:38
  149.7 4.1 %copy.42 = bf16[4,2,128,4,256]{4,2,0,3,1:T(8,128)(2,1)} copy(bf16[4,2,128,4,256]{2,1,0,4,3:T(2,128)(2,1)S(1)} %reshape.46) | data formatting | bytes 4194304 | tf_op jit(solution)/shard_map/reshape | solution.py:38
  153.8 22.8 %all-gather.9.cloned.1.call-done = bf16[4,2,128,16,1,64]{2,5,4,3,0,1:T(8,128)(2,1)} async-done(((bf16[4,1,128,16,1,64]{2,5,4,3,0,1:T(8,128)(2,1)}), bf16[4,2,128,16,1,64]{2,5,4,3,0,1:T(8,128)(2,1)}) %all-gather.9.cloned.1.call-update) | async-done | bytes 2097168 | tf_op jit(solution)/shard_map/all_gather | solution.py:34
  176.6 3.7 %copy.48 = bf16[4,2,128,16,1,64]{2,1,0,5,3,4:T(2,128)(2,1)S(1)} copy(bf16[4,2,128,16,1,64]{2,5,4,3,0,1:T(8,128)(2,1)} %all-gather.9.cloned.1.call-done) | data formatting | bytes 4194304 | tf_op jit(solution)/shard_map/all_gather | solution.py:34
  180.4 2.8 %reshape.50 = bf16[1024,1024]{0,1:T(8,128)(2,1)} reshape(bf16[4,2,128,16,1,64]{2,1,0,5,3,4:T(2,128)(2,1)S(1)} %copy.48) | data formatting | bytes 4194304 | tf_op jit(solution)/shard_map/reshape | solution.py:35
  183.2 7.9 %bitcast_reduce_fusion.1 = (f32[16,1792]{1,0:T(8,128)S(1)}, f32[16,1792]{1,0:T(8,128)S(1)}) fusion(bf16[1024,1792]{1,0:T(8,128)(2,1)} %all-gather.5.cloned.1.call-done, bf16[1024,1024]{0,1:T(8,128)(2,1)} %reshape.50, bf16[1024,1792]{1,0:T(8,128)(2,1)} %all-gather.7.cloned.1.call-done), kind=kOutput, calls=%fused_computation.1 | convolution fusion | flops 3765379072 | bytes 9666560 | tf_op jit(solution)/shard_map/dot_general | solution.py:46
  191.2 0.8 pad_maximum_fusion
  192.0 6.7 %all-to-all-start.4 = ((f32[1,2,8,2,1792]{4,3,1,0,2:T(2,128)}), f32[1,2,8,2,1792]{4,3,1,0,2:T(2,128)S(1)}, u32[]{:S(2)}, u32[]{:S(2)}) async-start(f32[1,2,8,2,1792]{4,3,1,0,2:T(2,128)} %pad_maximum_fusion), calls=%async_computation.5 | async-start | bytes 458752 | tf_op jit(solution)/shard_map/all_to_all | solution.py:50
  198.8 9.8 %all-to-all-done.4 = f32[1,2,8,2,1792]{4,3,1,0,2:T(2,128)S(1)} async-done(((f32[1,2,8,2,1792]{4,3,1,0,2:T(2,128)}), f32[1,2,8,2,1792]{4,3,1,0,2:T(2,128)S(1)}, u32[]{:S(2)}, u32[]{:S(2)}) %all-to-all-start.4) | async-done | bytes 229408 | tf_op jit(solution)/shard_map/all_to_all | solution.py:50
  208.8 0.8 reshape.60
  209.6 6.4 %all-to-all-start.5 = ((f32[64,1,224]{2,1,0:T(1,128)}), f32[64,1,224]{2,1,0:T(1,128)S(1)}, u32[]{:S(2)}, u32[]{:S(2)}) async-start(f32[64,1,224]{2,1,0:T(1,128)} %reshape.60), calls=%async_computation.6 | async-start | bytes 131072 | tf_op jit(solution)/shard_map/all_to_all | solution.py:56
  216.1 9.4 %all-to-all-done.5 = f32[64,1,224]{2,1,0:T(1,128)S(1)} async-done(((f32[64,1,224]{2,1,0:T(1,128)}), f32[64,1,224]{2,1,0:T(1,128)S(1)}, u32[]{:S(2)}, u32[]{:S(2)}) %all-to-all-start.5) | async-done | bytes 57376 | tf_op jit(solution)/shard_map/all_to_all | solution.py:56
  225.5 0.5 broadcast.3
  226.0 0.8 reduce.7
  226.8 0.2 reshape.61
  227.1 0.6 copy.51
  227.7 3.4 %all-to-all-start.2 = ((bf16[4,128,256]{2,1,0:T(8,128)(2,1)}), bf16[4,128,256]{2,1,0:T(8,128)(2,1)S(1)}, u32[]{:S(2)}, u32[]{:S(2)}) async-start(bf16[4,128,256]{2,1,0:T(8,128)(2,1)} %bitcast.62), calls=%async_computation.3 | async-start | bytes 524288 | tf_op jit(solution)/shard_map/all_to_all | solution.py:42
  231.1 1.4 negate_multiply_fusion
  232.5 4.1 %all-to-all-done.2 = bf16[4,128,256]{2,1,0:T(8,128)(2,1)S(1)} async-done(((bf16[4,128,256]{2,1,0:T(8,128)(2,1)}), bf16[4,128,256]{2,1,0:T(8,128)(2,1)S(1)}, u32[]{:S(2)}, u32[]{:S(2)}) %all-to-all-start.2) | async-done | bytes 262176 | tf_op jit(solution)/shard_map/all_to_all | solution.py:42
  236.6 0.2 copy.43
  236.8 0.9 copy.53
  (30 shorter events, 1.1 us)
Async XLA Ops:
  7.2 16.9 %copy-start = (s32[32,3584]{1,0:T(8,128)S(1)}, s32[32,3584]{1,0:T(8,128)}, u32[]{:S(2)}) copy-start(s32[32,3584]{1,0:T(8,128)} %param.9) | copy-start | bytes 1376260
  7.2 17.0 %copy-start.2 = (s32[64,3584]{1,0:T(8,128)S(1)}, s32[64,3584]{1,0:T(8,128)}, u32[]{:S(2)}) copy-start(s32[64,3584]{1,0:T(8,128)} %param.7) | copy-start | bytes 2752516
  7.2 77.5 %all-gather.7.cloned.1.call-start = ((), (), s32[]{:S(2)}) async-start(), calls=%async_computation.8 | async-start | bytes 4587520 | tf_op jit(solution)/shard_map/all_gather | solution.py:31
  21.8 10.9 %copy-start.1 = (bf16[128,4096]{1,0:T(8,128)(2,1)S(1)}, bf16[128,4096]{1,0:T(8,128)(2,1)}, u32[]{:S(2)}) copy-start(bf16[128,4096]{1,0:T(8,128)(2,1)} %param.5) | copy-start | bytes 3145732
  23.1 114.9 %all-gather.5.cloned.1.call-start = ((), (), s32[]{:S(2)}) async-start(), calls=%async_computation.7 | async-start | bytes 4128768 | tf_op jit(solution)/shard_map/all_gather | solution.py:30
  32.6 144.0 %all-gather.9.cloned.1.call-start = ((), (), s32[]{:S(2)}) async-start(), calls=%async_computation.10 | async-start | bytes 3145728 | tf_op jit(solution)/shard_map/all_gather | solution.py:34
  58.9 168.8 %reduce-scatter.2.cloned.1.call-start = ((), (), s32[]{:S(2)}) async-start(), calls=%async_computation.9 | async-start | bytes 2359296 | tf_op jit(solution)/shard_map/reduce_scatter | solution.py:41
  192.0 16.5 %all-to-all-start.4 = ((f32[1,2,8,2,1792]{4,3,1,0,2:T(2,128)}), f32[1,2,8,2,1792]{4,3,1,0,2:T(2,128)S(1)}, u32[]{:S(2)}, u32[]{:S(2)}) async-start(f32[1,2,8,2,1792]{4,3,1,0,2:T(2,128)} %pad_maximum_fusion), calls=%async_computation.5 | async-start | bytes 458752 | tf_op jit(solution)/shard_map/all_to_all | solution.py:50
  209.6 15.8 %all-to-all-start.5 = ((f32[64,1,224]{2,1,0:T(1,128)}), f32[64,1,224]{2,1,0:T(1,128)S(1)}, u32[]{:S(2)}, u32[]{:S(2)}) async-start(f32[64,1,224]{2,1,0:T(1,128)} %reshape.60), calls=%async_computation.6 | async-start | bytes 131072 | tf_op jit(solution)/shard_map/all_to_all | solution.py:56
  227.7 8.9 %all-to-all-start.2 = ((bf16[4,128,256]{2,1,0:T(8,128)(2,1)}), bf16[4,128,256]{2,1,0:T(8,128)(2,1)S(1)}, u32[]{:S(2)}, u32[]{:S(2)}) async-start(bf16[4,128,256]{2,1,0:T(8,128)(2,1)} %bitcast.62), calls=%async_computation.3 | async-start | bytes 524288 | tf_op jit(solution)/shard_map/all_to_all | solution.py:42
Sparse Core Ops, SparseCore 0:
  23.2 61.3 all-gather.6
  86.4 51.5 all-gather.4
  139.8 36.7 all-gather.8
  179.1 39.3 reduce-scatter.1

commit v2 on v1

v2 whole, which is shorter than its diff:
```python
import jax
import jax.numpy as jnp
from jax import lax
from jax.experimental import pallas as pl
from jax.experimental.pallas import tpu as pltpu
from jax.sharding import PartitionSpec as P

NZ, NL, NX, NH, NK = 8, 2, 4, 2, 2
MESH = pl.DeviceIdType.MESH
F32, BF16 = jnp.float32, jnp.bfloat16
Z_OFF = (0, 1, 7, 2, 6, 3, 5, 4)
Z_INV = (0, 2, 1, 4, 3, 6, 5, 7)
X_OFF = (0, 1, 3, 2)
X_INV = (0, 2, 1, 3)


def kernel(
    act_ref, go_ref, codes_ref, scales_ref, zeros_ref,
    out_ref, log_ref, zero_ref,
    act_v, codes_v, scales_v, zeros_v, scale32, fsend, frecv, wbuf, wsend, gbuf, act_t, asend, abuf, obuf, krecv, ybuf, yrecv, yown, xrecv,
    fin, lacc, lsent, lrecv,
    ins, zs, zr, xs, xr, ys, yr, as_, ar, ks, kr, os_, or_, fs, fr, ls, lr, es, er,
):
    dp, tensor = lax.axis_index("dp"), lax.axis_index("tensor")
    z, l, x = dp // (NL * NX), (dp // NX) % NL, dp % NX
    h, k = tensor // NK, tensor % NK
    rows, cols = codes_ref.shape
    tokens = go_ref.shape[0]
    half = cols // NL
    chunk = NL * rows
    nt = NX * tokens
    quarter = lacc.shape[2]

    def at(z_=z, l_=l, x_=x, h_=h, k_=k):
        return ((z_ * NL + l_) * NX + x_, h_ * NK + k_)

    direct = at(l_=1 - l)
    wrap = at(l_=1 - l, h_=1 - h)
    across = at(h_=1 - h)
    core = at(k_=1 - k)
    xs_of = [at(x_=(x + o) % NX) for o in X_OFF]
    zs_of = [at(z_=(z + o) % NZ) for o in Z_OFF]

    def copy(src, dst, send, recv, device):
        return pltpu.make_async_remote_copy(
            src_ref=src, dst_ref=dst, send_sem=send, recv_sem=recv,
            device_id=device, device_id_type=MESH,
        )

    def send(src, dst, s, r, device):
        copy(src, dst, s, r, device).start()

    def all_sent(ref, s):
        copy(ref, ref, s, s, core).wait_send()

    def arrived(dst, s, r):
        copy(dst, dst, s, r, core).wait_recv()

    own_cols = pl.ds(pl.multiple_of(l * half, 128), half)
    other_cols = pl.ds(pl.multiple_of((1 - l) * half, 128), half)
    group = dp // 2
    base = pl.multiple_of(group // 16 * 16, 16)
    barrier = pltpu.get_barrier_semaphore()
    loads = [
        pltpu.make_async_copy(src, dst, ins.at[i])
        for i, (src, dst) in enumerate((
            (scales_ref.at[pl.ds(base, 16), :], scales_v),
            (zeros_ref.at[pl.ds(base, 16), :], zeros_v),
            (codes_ref.at[:, other_cols], codes_v.at[1]),
            (codes_ref.at[:, own_cols], codes_v.at[0]),
            (act_ref, act_v),
            (go_ref.at[:, own_cols], gbuf.at[0:tokens, :]),
        ))
    ]
    for load in loads:
        load.start()
    partners = zs_of[1:3] + xs_of[1:] + [direct, wrap, core]
    for device in partners:
        pl.semaphore_signal(barrier, inc=1, device_id=device, device_id_type=MESH)
    lows = NZ // NL
    is_mine = z // lows == l
    part_rows = (
        pl.multiple_of(l * rows, rows),
        pl.multiple_of((1 - l) * rows, rows),
    )
    loads[0].wait()
    loads[1].wait()
    scale32[...] = scales_v[...].astype(F32)

    def dequantized(side, columns):
        scale = scale32[pl.ds(group - base, 1), columns]
        zero = zeros_v[pl.ds(group - base, 1), columns]
        return (scale * (codes_v[side] - zero).astype(F32)).astype(BF16)

    loads[2].wait()
    wsend[...] = dequantized(1, other_cols)
    loads[3].wait()
    wbuf[pl.ds(part_rows[0], rows), :] = dequantized(0, own_cols)
    features = act_ref.shape[1]
    loads[4].wait()
    for c in range(0, features, 128):
        act_t[c:c + 128, :] = act_v[:, c:c + 128].T
    hrows = NZ // 2 * chunk
    my_half = pl.multiple_of(k * hrows, hrows)
    for i in range(NZ // 2):
        z_at = (z + jnp.where(k == 0, Z_OFF[i], Z_OFF[NZ // 2 + i])) % NZ
        for l_at in range(NL):
            for j in range(NX):
                first = pl.multiple_of(((z_at * NL + l_at) * NX + (x + X_OFF[j]) % NX) * rows, rows)
                piece = act_t[pl.ds(first, rows), :]
                place = i * chunk + l_at * rows
                if j:
                    asend[j - 1, place:place + rows, :] = piece
                else:
                    abuf[pl.ds(pl.multiple_of(my_half + place, rows), rows), 0:tokens] = piece

    pl.semaphore_wait(barrier, len(partners))

    def wrows(slot, part, sub=None):
        count = rows if sub is None else rows // 2
        return wbuf.at[pl.ds(slot * chunk + part_rows[part] + (sub or 0) * (rows // 2), count), :]

    def zcopy(step, part, sub, way):
        src = wrows(2 * step - way if step else 0, part, sub)
        dst = wrows(2 * (step + 1) - way if step < 3 else 7, part, sub)
        i = ((way * 4 + step) * 2 + part) * 2 + sub
        return src, dst, zs.at[0], zr.at[i], zs_of[1 + way]

    def zpass(step, part):
        for n in range(2):
            for way in range(2):
                sub = n if way == 0 else 1 - n
                if step:
                    arrived(*zcopy(step - 1, part, sub, way)[1:4])
                if step < 3 or n == 0:
                    send(*zcopy(step, part, sub, way))

    def zlast(part):
        for way in range(2):
            arrived(*zcopy(3, part, way, way)[1:4])

    def grows(slot, part, first=0, count=None):
        start = part * nt + slot * tokens + first
        return gbuf.at[start:start + (count or tokens), :]

    turn = tokens * 3 // 8

    def xcopy(kind, part, way):
        first, count = (0, turn) if (kind == 1) == (way == 1) else (turn, tokens - turn)
        if kind == 2:
            src, dst = grows(2 - way, part, first, count), grows(3, part, first, count)
        else:
            src = grows(0, 1, first, count) if part else go_ref.at[first:first + count, own_cols]
            dst = grows(2 - way, part, first, count)
        i = (way * 3 + kind) * 2 + part
        return src, dst, xs.at[0], xr.at[i], xs_of[1 + way]

    def xown(part):
        for kind in (0, 1):
            for way in range(2):
                send(*xcopy(kind, part, way))

    def xpass(part):
        for way in range(2):
            arrived(*xcopy(0, part, way)[1:4])
            send(*xcopy(2, part, way))

    def xwait(kind, part):
        for way in range(2):
            arrived(*xcopy(kind, part, way)[1:4])

    def ablock(first, count, half_at=None):
        start = my_half if half_at is None else half_at
        return abuf.at[pl.ds(start, hrows), first:first + count]

    send(wsend, wrows(0, 0), ys.at[0], yr.at[0], direct)
    zpass(0, 0)
    for j in range(1, NX):
        send(asend.at[j - 1], ablock(X_INV[j] * tokens, tokens), as_.at[0], ar.at[X_INV[j] - 1], xs_of[j])
    xown(0)

    lacc[...] = jnp.zeros_like(lacc)

    def mix(r0, nr, t0, n):
        r, t = slice(r0, r0 + nr), slice(t0, t0 + n)
        obuf[r, t] = lax.dot_general(
            wbuf[r, :], gbuf[t, :], (((1,), (1,)), ((), ())), preferred_element_type=F32
        ).astype(BF16)

    def sums(r0, nr, t0, n):
        r, t = slice(r0, r0 + nr), slice(t0, t0 + n)
        for cc in range(2):
            c = slice(cc * quarter, (cc + 1) * quarter)
            gw = jnp.dot(abuf[r, t], gbuf[t, c], preferred_element_type=F32)
            for piece in range(nr // rows):
                p = slice(piece * rows, (piece + 1) * rows)
                g = gw[p]
                w = wbuf[r0 + piece * rows:r0 + (piece + 1) * rows, c].astype(F32)
                slot, l_at = (r0 // rows + piece) // NL, piece % NL
                at_row = cc * 4 + l_at
                lacc[slot, at_row:at_row + 1, :] += jnp.sum(g * w, axis=0, keepdims=True)
                lacc[slot, at_row + 2:at_row + 3, :] += jnp.sum(g, axis=0, keepdims=True)

    def compute(r0, nr, t0, n):
        mix(r0, nr, t0, n)
        sums(r0, nr, t0, n)

    def z_at(slot):
        return (z + Z_OFF[slot]) % NZ

    early = (NX - 1) * tokens
    lanes = (slice(0, nt), slice(nt, nt + early), slice(nt + early, 2 * nt))
    into = (slice(0, nt), slice(0, early), slice(early, nt))

    def tile(buf, slot, part):
        return buf.at[slot * chunk:(slot + 1) * chunk, lanes[part]]

    def slot_of(z_to):
        off = (z_to - z + NZ) % NZ
        return jnp.where(off == 0, 0, jnp.where(off < 4, 2 * off - 1, jnp.where(off == 4, 7, 2 * (NZ - off))))

    def ycopy(src, dst_at, part, zp, device):
        dst = yrecv.at[dst_at, zp, :, into[part]]
        return copy(src, dst, os_.at[0], or_.at[(dst_at * 3 + part) * 2 + zp], device)

    def block(buf, slot):
        return buf.at[pl.ds(pl.multiple_of(slot * chunk, chunk), chunk), lanes[2]]

    def last_send():
        for n in range(4):
            slot = slot_of(n // 2 * 4 + 2 * (1 - k) + n % 2)
            copy(block(obuf, slot), block(krecv, slot), ks.at[0], kr.at[slot * 3 + 2], core).start()

    def last_drain():
        for n in range(4):
            slot = slot_of(n // 2 * 4 + 2 * k + n % 2)
            arrived(block(krecv, slot), ks.at[0], kr.at[slot * 3 + 2])
            total = block(obuf, slot)[...].astype(F32) + block(krecv, slot)[...].astype(F32)
            block(ybuf, slot)[...] = total.astype(BF16)
            ycopy(block(ybuf, slot), jnp.where(h == n // 2, 1, 2), 2, n % 2, at(l_=1 - l, h_=n // 2)).start()

    def ksend(slots, parts):
        for slot in slots:
            for part in parts:
                i = slot * 3 + part

                @pl.when((z_at(slot) // 2) % 2 != k)
                def _():
                    copy(tile(obuf, slot, part), tile(krecv, slot, part), ks.at[0], kr.at[i], core).start()

    def kdrain_one(slot, part):
        i = slot * 3 + part
        zz = z_at(slot)

        @pl.when((zz // 2) % 2 == k)
        def _():
            arrived(tile(krecv, slot, part), ks.at[0], kr.at[i])
            total = tile(obuf, slot, part)[...].astype(F32) + tile(krecv, slot, part)[...].astype(F32)
            tile(ybuf, slot, part)[...] = total.astype(BF16)
            zp = zz % 2
            src = tile(ybuf, slot, part)
            if part == 0:
                @pl.when(zz // 4 != h)
                def _():
                    ycopy(src, 0, part, zp, across).start()
            else:
                ycopy(src, jnp.where(zz // 4 == h, 1, 2), part, zp, at(l_=1 - l, h_=zz // 4)).start()

    def kdrain(slots, parts):
        for slot in slots:
            for part in parts:
                kdrain_one(slot, part)

    eighth = quarter // 2

    def folded(slot):
        return jnp.concatenate([lacc[slot, :, 0:eighth], lacc[slot, :, eighth:quarter]], axis=0)

    def lsend(slot):
        lsent[slot - 1, :, 0:eighth] = folded(slot).astype(BF16)
        send(lsent.at[slot - 1], lrecv.at[Z_INV[slot] - 1], ls.at[0], lr.at[Z_INV[slot] - 1], zs_of[slot])

    t1, t2, t3, t4 = 3 * tokens, 2 * tokens, 2 * tokens, tokens
    zpass(1, 0)
    send(go_ref.at[:, other_cols], grows(0, 1), ys.at[0], yr.at[1], direct)
    arrived(wrows(0, 1), ys.at[0], yr.at[0])
    zpass(0, 1)
    for j in range(1, NX):
        arrived(ablock(j * tokens, tokens), as_.at[0], ar.at[j - 1])
    send(ablock(0, nt), ablock(0, nt), as_.at[0], ar.at[3], core)
    send(ablock(0, nt), ablock(nt, nt), as_.at[0], ar.at[4], wrap)
    zpass(2, 0)
    xpass(0)
    zpass(1, 1)
    loads[5].wait()
    arrived(grows(0, 1), ys.at[0], yr.at[1])
    xown(1)
    xwait(1, 0)
    other_half = pl.multiple_of((1 - k) * hrows, hrows)
    arrived(ablock(0, nt, other_half), as_.at[0], ar.at[3])
    compute(0, 3 * chunk, 0, t1)
    zpass(3, 0)
    arrived(ablock(nt, nt), as_.at[0], ar.at[4])
    send(ablock(nt, nt), ablock(nt, nt), as_.at[0], ar.at[5], core)
    zpass(2, 1)
    xwait(2, 0)
    arrived(ablock(nt, nt, other_half), as_.at[0], ar.at[5])
    compute(0, 3 * chunk, t1, t2)
    ksend((0, 1, 2), (0,))
    xpass(1)
    compute(3 * chunk, 2 * chunk, 0, t1 + t2)
    ksend((3, 4), (0,))
    kdrain((0, 1, 2), (0,))
    zpass(3, 1)
    xwait(1, 1)
    compute(0, 5 * chunk, t1 + t2, t3)
    ksend((0, 1, 2, 3, 4), (1,))
    kdrain((3, 4), (0,))
    compute(5 * chunk, 2 * chunk, 0, t1 + t2 + t3)
    ksend((5, 6), (0, 1))
    kdrain((0, 1, 2, 3, 4), (1,))
    xwait(2, 1)
    mix(0, 7 * chunk, t1 + t2 + t3, t4)
    kdrain((5, 6), (0, 1))
    zlast(0)
    zlast(1)
    mix(7 * chunk, chunk, 0, 2 * nt)
    ksend((7,), (0, 1))
    last_send()
    sums(0, 7 * chunk, t1 + t2 + t3, t4)
    for s in range(1, 7):
        lsend(s)
    kdrain((7,), (0, 1))
    last_drain()
    sums(7 * chunk, chunk, 0, 2 * nt)
    lsend(7)

    total = folded(0)
    for s in range(1, NZ):
        arrived(lrecv.at[s - 1], ls.at[0], lr.at[s - 1])
        total += lrecv[s - 1, :, 0:eighth].astype(F32)
    factors = []
    for side in range(2):
        for cc in range(2):
            columns = pl.ds(pl.multiple_of(l * half + cc * quarter, 128), quarter)
            factors.append(jnp.ones((2, eighth), F32))
            for l_at in range(NL):
                scale = scale32[pl.ds((z * NL + l_at) * 2 + x // 2 - base, 1), columns]
                factors.append(-scale[:, side * eighth:(side + 1) * eighth])
    total *= jnp.concatenate(factors, axis=0)
    width = log_ref.shape[1]
    for j in range(fsend.shape[0]):
        cc, m = j // (quarter // width), j % (quarter // width)
        side, m = m // (eighth // width), m % (eighth // width)
        fsend[j, :, 0:width] = total[side * 8 + cc * 4:side * 8 + cc * 4 + 4, m * width:(m + 1) * width]
    here = z * NX + x
    for n in range(lows * NL * NX):
        zq, l_to, x_to = (z + n // (NL * NX)) % lows, (l + n // NX) % NL, (x + n) % NX
        src, dst = fsend.at[(zq * NL + l_to) * NX + x_to], frecv.at[here]
        device = at(z_=l * lows + zq, l_=l_to, x_=x_to)
        if n:
            copy(src, dst, es.at[0], er.at[0], device).start()
        else:
            @pl.when(jnp.logical_not(is_mine))
            def _():
                copy(src, dst, es.at[0], er.at[0], device).start()

            @pl.when(is_mine)
            def _():
                pltpu.make_async_copy(src, dst, er.at[0]).start()

    q = h * NK + k
    for part in (1, 2):
        for zp in range(2):
            slot = slot_of(2 * q + zp)
            if part == 1:
                arrived(yrecv.at[0, zp], os_.at[0], or_.at[zp])
            for src in (1, 2):
                arrived(yrecv.at[src, zp, :, into[part]], os_.at[0], or_.at[(src * 3 + part) * 2 + zp])
            total = ybuf[pl.ds(pl.multiple_of(slot * chunk, chunk), chunk), into[part]].astype(F32)
            for src in range(3):
                total += yrecv[src, zp, :, into[part]].astype(F32)
            yown[zp, :, into[part]] = total.astype(BF16)
            for j in (1, 2) if part == 1 else (3,):
                i = (j - 1) * 2 + zp
                r = (X_INV[j] - 1) * 2 + zp
                send(yown.at[zp, :, j * tokens:(j + 1) * tokens], xrecv.at[X_INV[j] - 1, zp], fs.at[0], fr.at[r], xs_of[j])

    for zp in range(2):
        for j in range(NX):
            if j:
                arrived(xrecv.at[j - 1, zp], fs.at[0], fr.at[(j - 1) * 2 + zp])
            x_at = (x + X_OFF[j]) % NX
            for l_at in range(NL):
                p = slice(l_at * rows, (l_at + 1) * rows)
                piece = xrecv[j - 1, zp, p, :] if j else yown[zp, p, 0:tokens]
                first = ((zp * NL + l_at) * NX + x_at) * rows
                fin[pl.ds(pl.multiple_of(first, rows), rows), :] = piece
    for c in range(0, fin.shape[0], 128):
        out_ref[:, c:c + 128] = fin[c:c + 128, :].T

    copy(frecv, frecv, es.at[0], er.at[0], core).wait_recv()
    for zj in range(NZ):
        for pair in range(NX // 2):
            four = frecv[zj * NX + 2 * pair] + frecv[zj * NX + 2 * pair + 1]
            for l_at in range(NL):
                g = (zj * NL + l_at) * 2 + pair
                log_ref[g:g + 1, :] = four[l_at:l_at + 1, 0:width]
                zero_ref[g:g + 1, :] = four[2 + l_at:3 + l_at, 0:width]

    all_sent(wbuf.at[0:7 * chunk, :], zs.at[0])
    all_sent(gbuf.at[0:6 * tokens, :], xs.at[0])
    all_sent(wsend, ys.at[0])
    all_sent(grows(0, 0), ys.at[0])
    all_sent(asend, as_.at[0])
    for _ in range(3):
        all_sent(ablock(0, nt), as_.at[0])
    all_sent(obuf.at[0:4 * chunk, :], ks.at[0])
    all_sent(ybuf.at[0:3 * chunk, :], os_.at[0])
    all_sent(xrecv, fs.at[0])
    all_sent(lsent, ls.at[0])
    copy(frecv.at[0:NZ * NX - 1], frecv.at[0:NZ * NX - 1], es.at[0], er.at[0], core).wait_send()

    @pl.when(jnp.logical_not(is_mine))
    def _():
        copy(frecv.at[0], frecv.at[0], es.at[0], er.at[0], core).wait_send()


def on_device(activations, grad_out, weight_codes, scales, zero_points):
    tokens, features = activations.shape
    rows, cols = weight_codes.shape
    half = cols // NL
    groups = scales.shape[0]
    chunk, nt = NL * rows, NX * tokens
    vmem = pl.BlockSpec(memory_space=pltpu.VMEM)
    dma = pltpu.SemaphoreType.DMA
    width = cols // (NZ * NL * NX)
    hbm = pl.BlockSpec(memory_space=pltpu.HBM)
    out, log_sums, zero_sums = pl.pallas_call(
        kernel,
        out_shape=(
            jax.ShapeDtypeStruct((tokens, features // (NH * NK)), BF16),
            jax.ShapeDtypeStruct((groups, width), F32),
            jax.ShapeDtypeStruct((groups, width), F32),
        ),
        in_specs=[hbm] * 5,
        out_specs=(vmem, vmem, vmem),
        scratch_shapes=[
            pltpu.VMEM((tokens, features), BF16),
            pltpu.VMEM((2, rows, half), jnp.int32),
            pltpu.VMEM((16, cols), BF16),
            pltpu.VMEM((16, cols), jnp.int32),
            pltpu.VMEM((16, cols), F32),
            pltpu.VMEM((half // width, 4, 128), F32),
            pltpu.VMEM((NZ * NX, 4, 128), F32),
            pltpu.VMEM((NZ * chunk, half), BF16),
            pltpu.VMEM((rows, half), BF16),
            pltpu.VMEM((NL * nt, half), BF16),
            pltpu.VMEM((features, tokens), BF16),
            pltpu.VMEM((NX - 1, NZ // 2 * chunk, tokens), BF16),
            pltpu.VMEM((NZ * chunk, NL * nt), BF16),
            pltpu.VMEM((NZ * chunk, NL * nt), BF16),
            pltpu.VMEM((NZ * chunk, NL * nt), BF16),
            pltpu.VMEM((NZ * chunk, NL * nt), BF16),
            pltpu.VMEM((3, 2, chunk, nt), BF16),
            pltpu.VMEM((2, chunk, nt), BF16),
            pltpu.VMEM((NX - 1, 2, chunk, tokens), BF16),
            pltpu.VMEM((2 * NX * chunk, tokens), BF16),
            pltpu.VMEM((NZ, 8, half // 2), F32),
            pltpu.VMEM((NZ - 1, 16, 512), BF16),
            pltpu.VMEM((NZ - 1, 16, 512), BF16),
            dma((6,)),
            dma((1,)), dma((32,)),
            dma((1,)), dma((12,)),
            dma((1,)), dma((2,)),
            dma((1,)), dma((6,)),
            dma((1,)), dma((24,)),
            dma((1,)), dma((18,)),
            dma((1,)), dma((6,)),
            dma((1,)), dma((7,)),
            dma((1,)), dma((1,)),
        ],
        compiler_params=pltpu.CompilerParams(
            collective_id=0, has_side_effects=True, vmem_limit_bytes=63 * 2**20
        ),
        cost_estimate=pl.CostEstimate(
            flops=4 * NZ * chunk * NL * nt * half, bytes_accessed=4 * 2**20, transcendentals=0
        ),
    )(activations, grad_out, weight_codes, scales, zero_points)

    return (out, log_sums[:, None, :], zero_sums[:, None, :])


def solution(mesh):
    in_specs = (
        P("dp", None),
        P("dp", "tensor"),
        P("dp", "tensor"),
        P(None, "tensor"),
        P(None, "tensor"),
    )
    out_specs = (P("dp", "tensor"), P(None, "tensor", "dp"), P(None, "tensor", "dp"))
    return jax.shard_map(
        on_device, mesh=mesh, in_specs=in_specs, out_specs=out_specs, check_vma=False
    )
```

time: 247 us -> 71 us (0.29)
  waiting for transfers between devices: 125 us -> 0 us
  Pallas kernels: 0 us -> 66.6 us
  blocking collectives: 46.5 us -> 0 us
  local copies, waits for them, and re-layouts: 21.3 us -> 3.01 us
  starting transfers between devices: 16.7 us -> 0 us
  matrix products: 16.3 us -> 0 us
  between operations: 14 us -> 0.65 us
  other arithmetic: 4.14 us -> 0 us
    all_gather x3 -> x0, waiting for transfers between devices: 102 us -> none  [the longest x1 53.3 us: on_device(): w = lax.all_gather(w, 'z', axis=0, tiled=True)]
    pallas_call x0 -> x1, Pallas kernels: none -> 66.6 us  [on_device(): pl.pallas_call(kernel, out_shape=(jax.ShapeDtypeStruct((tokens, features...]
    all_to_all x3 -> x0, blocking collectives: 46.5 us -> none  [the longest x1 25.4 us: on_device(): act = lax.all_to_all(act, 'x', 2, 0, tiled=False)]
    all_to_all x3 -> x0, waiting for transfers between devices: 23.3 us -> none  [the longest x1 9.76 us: on_device(): parts = lax.all_to_all(parts, 'z', 1, 0, tiled=False).sum(axis=0)]
    all_to_all x3 -> x0, starting transfers between devices: 16.5 us -> none  [the longest x1 6.73 us: on_device(): parts = lax.all_to_all(parts, 'z', 1, 0, tiled=False).sum(axis=0)]
    dot_general x2 -> x0, matrix products: 16.3 us -> none  [the longest x1 8.45 us: on_device(): lax.dot_general(go, w, (((1,), (1,)), ((), ())), preferred_element_type=j...]
    reshape x4 -> x0, local copies, waits for them, and re-layouts: 10.2 us -> none  [the longest x2 7.33 us: on_device(): out.astype(jnp.bfloat16).reshape(NX, NL, tokens, NH * NK, 2 * NL * rows)]
    all_gather x1 -> x0, local copies, waits for them, and re-layouts: 3.75 us -> none  [on_device(): act = lax.all_gather(act, 'l', axis=1, tiled=False)]
  transfers between devices with their start and end apart: 7 -> 0, of which waited for: 6 -> 0; matrix products, arithmetic and copies ran while one was open for 15% -> 0% of each run, Pallas kernels for 0% -> 0%
where the time goes in v2:
time: 71 us; the launch traced here: 70.3 us
  Pallas kernels  66.6 us (94%)
  local copies, waits for them, and re-layouts  3.01 us (4%)
    pallas_call x1, Pallas kernels, on_device(): pl.pallas_call(kernel, out_shape=(jax.ShapeDtypeStruct((tokens, features...  66.6 us
    unnamed x7, local copies, waits for them, and re-layouts  3.01 us

profile of v2, /device:TPU:1, one launch (start us, length us, event | category | flops | bytes accessed | tf_op | source)
XLA Modules:
  0.0 70.3 jit_solution(3460821921611834722)
XLA Ops:
  0.6 66.6 %shard_map.76 = (bf16[128,1024]{1,0:T(8,128)(2,1)}, f32[32,56]{1,0:T(8,128)}, f32[32,56]{1,0:T(8,128)}) custom-call(bf16[128,4096]{1,0:T(8,128)(2,1)} %act_ref.1, bf16[128,3584]{1,0:T(8,128)(2,1)} %go_ref.1, s32[64,3584]{1,0:T(8,128)} %codes_ref.1, bf16[32,3584]{1,0:T(8,128)(2,1)} %scales_ref.1, s32[32,3584]{1,0:T(8,128)} %zeros_ref.1), custom_call_target="tpu_custom_call" | custom-call | flops 7516192768 | bytes 4194304 | tf_op jit(solution)/shard_map/pallas_call | solution.py:439
  67.3 0.0 copy-start.1
  67.3 1.7 %copy.13 = bf16[128,1024]{1,0:T(8,128)(2,1)} copy(bf16[128,1024]{1,0:T(8,128)(2,1)} %get-tuple-element.15) | data formatting | bytes 524288
  69.0 0.0 copy-done.1
  69.0 0.0 copy-start
  69.0 0.6 copy.14
  69.6 0.1 copy-done
  69.7 0.6 copy.15
Async XLA Ops:
  67.3 1.7 %copy-start.1 = (f32[32,56]{1,0:T(8,128)S(1)}, f32[32,56]{1,0:T(8,128)}, u32[]{:S(2)}) copy-start(f32[32,56]{1,0:T(8,128)} %get-tuple-element.7) | copy-start | bytes 21508
  69.0 0.7 %copy-start = (f32[32,56]{1,0:T(8,128)S(1)}, f32[32,56]{1,0:T(8,128)}, u32[]{:S(2)}) copy-start(f32[32,56]{1,0:T(8,128)} %get-tuple-element.8) | copy-start | bytes 21508

commit v3 on v2

--- a/solution.py
+++ b/solution.py
@@ -321,19 +321,19 @@
     kdrain((0, 1, 2, 3, 4), (1,))
     xwait(2, 1)
     mix(0, 7 * chunk, t1 + t2 + t3, t4)
+    sums(0, 7 * chunk, t1 + t2 + t3, t4)
+    for s in range(1, 7):
+        lsend(s)
     kdrain((5, 6), (0, 1))
     zlast(0)
     zlast(1)
+    sums(7 * chunk, chunk, 0, 2 * nt)
+    lsend(7)
     mix(7 * chunk, chunk, 0, 2 * nt)
     ksend((7,), (0, 1))
     last_send()
-    sums(0, 7 * chunk, t1 + t2 + t3, t4)
-    for s in range(1, 7):
-        lsend(s)
     kdrain((7,), (0, 1))
     last_drain()
-    sums(7 * chunk, chunk, 0, 2 * nt)
-    lsend(7)
 
     total = folded(0)
     for s in range(1, NZ):

time: 71 us -> 68.7 us (0.968)
  Pallas kernels: 66.6 us -> 64.9 us
    pallas_call x1, Pallas kernels: 66.6 us -> 64.9 us  [on_device(): pl.pallas_call(kernel, out_shape=(jax.ShapeDtypeStruct((tokens, features...]
where the time goes in v3:
time: 68.7 us; the launch traced here: 68.5 us
  Pallas kernels  64.9 us (94%)
  local copies, waits for them, and re-layouts  3.01 us (4%)
    pallas_call x1, Pallas kernels, on_device(): pl.pallas_call(kernel, out_shape=(jax.ShapeDtypeStruct((tokens, features...  64.9 us
    unnamed x7, local copies, waits for them, and re-layouts  3.01 us

profile of v3, /device:TPU:1, one launch (start us, length us, event | category | flops | bytes accessed | tf_op | source)
XLA Modules:
  0.0 68.5 jit_solution(10389504370675454373)
XLA Ops:
  0.6 64.9 %shard_map.76 = (bf16[128,1024]{1,0:T(8,128)(2,1)}, f32[32,56]{1,0:T(8,128)}, f32[32,56]{1,0:T(8,128)}) custom-call(bf16[128,4096]{1,0:T(8,128)(2,1)} %act_ref.1, bf16[128,3584]{1,0:T(8,128)(2,1)} %go_ref.1, s32[64,3584]{1,0:T(8,128)} %codes_ref.1, bf16[32,3584]{1,0:T(8,128)(2,1)} %scales_ref.1, s32[32,3584]{1,0:T(8,128)} %zeros_ref.1), custom_call_target="tpu_custom_call" | custom-call | flops 7516192768 | bytes 4194304 | tf_op jit(solution)/shard_map/pallas_call | solution.py:439
  65.5 0.0 copy-start.1
  65.5 1.7 %copy.13 = bf16[128,1024]{1,0:T(8,128)(2,1)} copy(bf16[128,1024]{1,0:T(8,128)(2,1)} %get-tuple-element.15) | data formatting | bytes 524288
  67.2 0.0 copy-done.1
  67.2 0.0 copy-start
  67.2 0.6 copy.14
  67.8 0.1 copy-done
  67.9 0.6 copy.15
Async XLA Ops:
  65.5 1.7 %copy-start.1 = (f32[32,56]{1,0:T(8,128)S(1)}, f32[32,56]{1,0:T(8,128)}, u32[]{:S(2)}) copy-start(f32[32,56]{1,0:T(8,128)} %get-tuple-element.7) | copy-start | bytes 21508
  67.2 0.7 %copy-start = (f32[32,56]{1,0:T(8,128)S(1)}, f32[32,56]{1,0:T(8,128)}, u32[]{:S(2)}) copy-start(f32[32,56]{1,0:T(8,128)} %get-tuple-element.8) | copy-start | bytes 21508

commit v4 on v3

--- a/solution.py
+++ b/solution.py
@@ -143,7 +143,7 @@
         start = part * nt + slot * tokens + first
         return gbuf.at[start:start + (count or tokens), :]
 
-    turn = tokens * 3 // 8
+    turn = tokens // 2
 
     def xcopy(kind, part, way):
         first, count = (0, turn) if (kind == 1) == (way == 1) else (turn, tokens - turn)

time: 68.7 us -> 68.5 us (level)
  no operation moved by 1% of the time
where the time goes in v4:
time: 68.5 us; the launch traced here: 68.3 us
  Pallas kernels  64.7 us (94%)
  local copies, waits for them, and re-layouts  3.01 us (4%)
    pallas_call x1, Pallas kernels, on_device(): pl.pallas_call(kernel, out_shape=(jax.ShapeDtypeStruct((tokens, features...  64.7 us
    unnamed x7, local copies, waits for them, and re-layouts  3.01 us

profile of v4, /device:TPU:1, one launch (start us, length us, event | category | flops | bytes accessed | tf_op | source)
XLA Modules:
  0.0 68.3 jit_solution(13806857297877009914)
XLA Ops:
  0.6 64.7 %shard_map.76 = (bf16[128,1024]{1,0:T(8,128)(2,1)}, f32[32,56]{1,0:T(8,128)}, f32[32,56]{1,0:T(8,128)}) custom-call(bf16[128,4096]{1,0:T(8,128)(2,1)} %act_ref.1, bf16[128,3584]{1,0:T(8,128)(2,1)} %go_ref.1, s32[64,3584]{1,0:T(8,128)} %codes_ref.1, bf16[32,3584]{1,0:T(8,128)(2,1)} %scales_ref.1, s32[32,3584]{1,0:T(8,128)} %zeros_ref.1), custom_call_target="tpu_custom_call" | custom-call | flops 7516192768 | bytes 4194304 | tf_op jit(solution)/shard_map/pallas_call | solution.py:439
  65.3 0.0 copy-start.1
  65.3 1.7 %copy.13 = bf16[128,1024]{1,0:T(8,128)(2,1)} copy(bf16[128,1024]{1,0:T(8,128)(2,1)} %get-tuple-element.15) | data formatting | bytes 524288
  67.0 0.0 copy-done.1
  67.0 0.0 copy-start
  67.0 0.6 copy.14
  67.6 0.1 copy-done
  67.7 0.6 copy.15
Async XLA Ops:
  65.3 1.7 %copy-start.1 = (f32[32,56]{1,0:T(8,128)S(1)}, f32[32,56]{1,0:T(8,128)}, u32[]{:S(2)}) copy-start(f32[32,56]{1,0:T(8,128)} %get-tuple-element.7) | copy-start | bytes 21508
  67.0 0.7 %copy-start = (f32[32,56]{1,0:T(8,128)S(1)}, f32[32,56]{1,0:T(8,128)}, u32[]{:S(2)}) copy-start(f32[32,56]{1,0:T(8,128)} %get-tuple-element.8) | copy-start | bytes 21508
